TPU v7x, 32 devices: a whole 2x2x4 slice. The times are simulated.
32 devices in a mesh: seq: 8 (over y, x, core), ch: 4 (over z).
Axes of the slice: x: 2, y: 2, z: 4, core: 2. Of those that a mesh axis runs over, the one named last changes fastest.
Arguments:
- tokens: bfloat16 [65536, 1024], P('seq', 'ch'), may hold values from -6 to 6
- gating: bfloat16 [65536, 1024], P('seq', 'ch'), may hold values from -6 to 6
- spectral_gain: float32 [32, 128, 1024], P(None, None, 'ch'), may hold values from 0.25 to 4
- device_gain: float32 [8, 1024], P(None, 'ch'), may hold values from 0.25 to 4
- retained: int32 [64], P('ch'), may hold values from 32 to 128, as said below
- block_weight: bfloat16 [4, 256, 256], replicated, may hold values from -0.375 to 0.375
- mix_weight: float32 [256, 4, 4], replicated, may hold values from -3 to 3
Outputs:
- channel_mixed: bfloat16 [65536, 1024], P(('seq', 'ch'))
Inputs may be any that keep to these rules, and one draw needn't show every extreme that they name: `retained`: in every aligned run of 8 channel groups at least one group has 128, the most, at a position drawn from the seed; the others lie between 32 and 128.
All inputs are finite; a program needn't handle non-finite values.
Results may differ from a plain program's by a relative error of at most 0.0049.
Values may be sent and summed in bfloat16 or wider, within the bound.
A program may use at most 128 MiB of HBM per device.

v0:
```python
import math

import jax
import jax.numpy as jnp
from jax import lax
from jax.sharding import PartitionSpec as P

GSZ = 16
B = 256
A = 32
KMAX = 128


def swapped(block, axis, stride):
    count = lax.axis_size(axis)
    route = []
    for low in range(count):
        high = low | 1 << stride
        if high != low and high < count:
            route += [(low, high), (high, low)]
    return lax.ppermute(block, axis, route)


def cosine_table(length):
    rows = jnp.arange(length, dtype=jnp.int32)[:, None].astype(jnp.float32)
    cols = jnp.arange(length, dtype=jnp.int32)[None, :].astype(jnp.float32)
    table = jnp.cos(math.pi * (2.0 * cols + 1.0) * rows / (2.0 * length)) * math.sqrt(2.0 / length)
    return jnp.where(rows == 0.0, table * math.sqrt(0.5), table)


def local(tokens, gating, spectral_gain, device_gain, retained, block_weight, mix_weight):
    high = lax.Precision.HIGHEST
    local_rows, local_width = tokens.shape
    devices = lax.axis_size("seq")
    levels = devices.bit_length() - 1
    band_table = cosine_table(B)[:KMAX]
    block_table = cosine_table(A)
    spectra = tokens.astype(jnp.float32).reshape(A, B, local_width)
    spectra = jnp.einsum("kb,abc->akc", band_table, spectra, precision=high)
    spectra = jnp.einsum("ja,akc->jkc", block_table, spectra, precision=high)
    group_keep = jnp.repeat(retained, GSZ)
    passband = jnp.arange(KMAX, dtype=jnp.int32)[:, None] < group_keep[None, :]
    spectra = spectra * jnp.where(passband[None], spectral_gain, 0.0)
    position = lax.axis_index("seq")
    for level in range(levels):
        angle = 0.6 + 0.1 * level
        partner = swapped(spectra, "seq", level)
        factor = jnp.where(
            jnp.right_shift(position, level) % 2 == 1, -math.cos(angle), math.cos(angle)
        )
        spectra = factor * spectra + math.sin(angle) * partner
    own_gain = lax.dynamic_slice_in_dim(device_gain, position, 1, 0)[0]
    spectra = spectra * own_gain[None, None, :]
    for level in range(levels):
        angle = 0.6 + 0.1 * level
        partner = swapped(spectra, "seq", level)
        factor = jnp.where(
            jnp.right_shift(position, level) % 2 == 1, -math.cos(angle), math.cos(angle)
        )
        spectra = factor * spectra + math.sin(angle) * partner
    spectra = jnp.einsum("ja,jkc->akc", block_table, spectra, precision=high)
    spectra = jnp.einsum("kb,akc->abc", band_table, spectra, precision=high)
    smoothed = spectra.reshape(local_rows, local_width)
    gated = (gating.astype(jnp.float32) * smoothed).astype(jnp.bfloat16)
    gathered = lax.all_to_all(gated, "ch", split_axis=0, concat_axis=1, tiled=True)
    row_count, full_width = gathered.shape
    blocks = block_weight.shape[0]
    block_size = block_weight.shape[1]
    gathered = gathered.reshape(row_count, blocks, block_size)
    first_section = jnp.einsum(
        "rid,ide->rie", gathered, block_weight, preferred_element_type=jnp.float32
    )
    result = jnp.einsum("rie,eki->rke", first_section, mix_weight, precision=high)
    return result.reshape(row_count, full_width).astype(jnp.bfloat16)


def solution(mesh):
    in_specs = (
        P("seq", "ch"),
        P("seq", "ch"),
        P(None, None, "ch"),
        P(None, "ch"),
        P("ch"),
        P(),
        P(),
    )
    out_specs = P(("seq", "ch"), None)
    return jax.shard_map(local, mesh=mesh, in_specs=in_specs, out_specs=out_specs, check_vma=False)
```

profile of v0, /device:TPU:0, one launch (start us, length us, event | category | flops | bytes accessed | tf_op | source)
XLA Modules:
  0.0 582.4 jit_solution(13130913963040967887)
XLA Ops:
  0.0 0.0 copy-start
  0.1 0.8 broadcast_in_dim.43
  0.8 0.1 lt.46
  1.0 0.0 copy-start.1
  1.0 4.7 fusion.18
  5.6 0.0 copy-done.1
  5.7 9.4 %fusion.8 = f32[32,128,256]{2,0,1:T(8,128)} fusion(f32[32,128,256]{2,1,0:T(8,128)S(1)} %copy-done.1, f32[128,32,256]{2,0,1:T(8,128)S(1)} %fusion.18, pred[128,256]{1,0:T(8,128)(4,1)S(1)} %iota_compare_fusion, f32[32]{0:T(128)S(1)} %iota_convert_fusion.1, f32[32]{0:T(128)S(1)} %add_multiply_fusion.2, pred[32]{0:T(512)(128)(4,1)S(1)} %broadcast_compare_fusion), kind=kOutput, calls=%fused_computation.10 | convolution fusion | flops 404755456 | bytes 12615968 | tf_op jit(solution)/shard_map/ja,akc->jkc/dot_general | solution.py:40
  15.0 0.5 collective-permute-start
  15.5 7.1 %collective-permute-done = f32[32,128,256]{2,0,1:T(8,128)} collective-permute-done((f32[32,128,256]{2,0,1:T(8,128)}, f32[32,128,256]{2,0,1:T(8,128)}, u32[]{:S(2)}, u32[]{:S(2)}) %collective-permute-start) | collective-permute-done | bytes 4194336 | tf_op jit(solution)/shard_map/ppermute | solution.py:21
  22.7 6.9 %multiply_add_fusion.3 = f32[32,128,256]{2,0,1:T(8,128)} fusion(f32[32,128,256]{2,0,1:T(8,128)} %collective-permute-done, f32[32,128,256]{2,0,1:T(8,128)} %fusion.8, f32[]{:T(128)S(6)} %select_n.59), kind=kLoop, calls=%fused_computation.20 | loop fusion | flops 3145728 | bytes 12582916 | tf_op jit(solution)/shard_map/add | solution.py:51
  29.6 2.9 collective-permute-start.1
  32.5 91.2 %collective-permute-done.1 = f32[32,128,256]{2,0,1:T(8,128)} collective-permute-done((f32[32,128,256]{2,0,1:T(8,128)}, f32[32,128,256]{2,0,1:T(8,128)}, u32[]{:S(2)}, u32[]{:S(2)}) %collective-permute-start.1) | collective-permute-done | bytes 4194336 | tf_op jit(solution)/shard_map/ppermute | solution.py:21
  123.7 6.9 %multiply_add_fusion.2 = f32[32,128,256]{2,0,1:T(8,128)} fusion(f32[32,128,256]{2,0,1:T(8,128)} %collective-permute-done.1, f32[32,128,256]{2,0,1:T(8,128)} %multiply_add_fusion.3, f32[]{:T(128)S(6)} %select_n.57), kind=kLoop, calls=%fused_computation.19 | loop fusion | flops 3145728 | bytes 12582916 | tf_op jit(solution)/shard_map/add | solution.py:51
  130.6 1.8 collective-permute-start.2
  132.4 0.7 constant_dynamic-slice_fusion
  133.1 89.9 %collective-permute-done.2 = f32[32,128,256]{2,0,1:T(8,128)} collective-permute-done((f32[32,128,256]{2,0,1:T(8,128)}, f32[32,128,256]{2,0,1:T(8,128)}, u32[]{:S(2)}, u32[]{:S(2)}) %collective-permute-start.2) | collective-permute-done | bytes 4194336 | tf_op jit(solution)/shard_map/ppermute | solution.py:21
  223.0 4.5 add_multiply_fusion
  227.5 0.1 collective-permute-start.3
  227.6 7.1 %collective-permute-done.3 = f32[32,128,256]{2,0,1:T(8,128)S(1)} collective-permute-done((f32[32,128,256]{2,0,1:T(8,128)S(1)}, f32[32,128,256]{2,0,1:T(8,128)S(1)}, u32[]{:S(2)}, u32[]{:S(2)}) %collective-permute-start.3) | collective-permute-done | bytes 4194336 | tf_op jit(solution)/shard_map/ppermute | solution.py:21
  234.7 1.5 multiply_add_fusion.1
  236.2 1.5 collective-permute-start.4
  237.7 91.2 %collective-permute-done.4 = f32[32,128,256]{2,0,1:T(8,128)S(1)} collective-permute-done((f32[32,128,256]{2,0,1:T(8,128)S(1)}, f32[32,128,256]{2,0,1:T(8,128)S(1)}, u32[]{:S(2)}, u32[]{:S(2)}) %collective-permute-start.4) | collective-permute-done | bytes 4194336 | tf_op jit(solution)/shard_map/ppermute | solution.py:21
  328.9 1.5 multiply_add_fusion
  330.3 1.5 collective-permute-start.5
  331.9 90.3 %collective-permute-done.5 = f32[32,128,256]{2,0,1:T(8,128)S(1)} collective-permute-done((f32[32,128,256]{2,0,1:T(8,128)S(1)}, f32[32,128,256]{2,0,1:T(8,128)S(1)}, u32[]{:S(2)}, u32[]{:S(2)}) %collective-permute-start.5) | collective-permute-done | bytes 4194336 | tf_op jit(solution)/shard_map/ppermute | solution.py:21
  422.2 4.0 fusion.9
  426.3 0.0 copy-start.2
  426.3 10.0 %fusion.5 = f32[32,256,256]{1,2,0:T(8,128)S(1)} fusion(f32[32,128,256]{2,0,1:T(8,128)S(1)} %fusion.9, f32[128]{0:T(128)S(1)} %slice.6, f32[256]{0:T(256)S(1)} %add_multiply_fusion.1, pred[128]{0:T(512)(128)(4,1)S(1)} %bitcast.40), kind=kOutput, calls=%fused_computation.6 | convolution fusion | flops 3221389312 | bytes 12584576 | tf_op jit(solution)/shard_map/kb,akc->abc/dot_general | solution.py:62
  436.2 0.0 copy-done.2
  436.3 3.5 fusion
  439.7 0.0 copy-start.3
  439.8 5.3 all-to-all-start
  445.1 0.0 copy-done.3
  445.1 0.3 copy.11
  445.3 91.8 %all-to-all-done = bf16[4,2048,256]{2,1,0:T(8,128)(2,1)} async-done(((bf16[4,2048,256]{2,1,0:T(8,128)(2,1)}), bf16[4,2048,256]{2,1,0:T(8,128)(2,1)}, u32[]{:S(2)}, u32[]{:S(2)}) %all-to-all-start) | async-done | bytes 4194336 | tf_op jit(solution)/shard_map/all_to_all | solution.py:65
  537.1 0.0 copy-done
  537.1 6.7 %fusion.1 = f32[4,2048,256]{2,1,0:T(8,128)} fusion(bf16[4,256,256]{2,1,0:T(8,128)(2,1)S(1)} %copy-done, bf16[4,2048,256]{2,1,0:T(8,128)(2,1)} %all-to-all-done), kind=kOutput, calls=%fused_computation.2 | convolution fusion | flops 1073741824 | bytes 13107200 | tf_op jit(solution)/shard_map/rid,ide->rie/dot_general | solution.py:70
  543.8 10.5 %copy.16 = f32[4,2048,256]{1,0,2:T(4,128)} copy(f32[4,2048,256]{2,1,0:T(8,128)} %fusion.1) | data formatting | bytes 16777216 | tf_op jit(solution)/shard_map/rid,ide->rie/dot_general | solution.py:70
  554.2 17.1 %convert_bitcast_fusion = bf16[2048,4,256]{0,1,2:T(4,128)(2,1)S(1)} fusion(f32[4,2048,256]{1,0,2:T(4,128)} %copy.16, f32[256,4,4]{2,1,0:T(4,128)S(1)} %copy.11), kind=kOutput, calls=%fused_computation.11 | convolution fusion | flops 102760448 | bytes 12599296 | tf_op jit(solution)/shard_map/rie,eki->rke/dot_general | solution.py:73
  571.3 4.3 copy.12
  575.6 6.4 %copy.13 = bf16[2048,1024]{1,0:T(8,128)(2,1)} copy(bf16[2048,1024]{0,1:T(8,128)(2,1)} %bitcast.35) | data formatting | bytes 8388608 | tf_op jit(solution)/shard_map/convert_element_type | solution.py:74
  (8 shorter events, 0.1 us)
Async XLA Ops:
  0.0 537.1 %copy-start = (bf16[4,256,256]{2,1,0:T(8,128)(2,1)S(1)}, bf16[4,256,256]{2,1,0:T(8,128)(2,1)}, u32[]{:S(2)}) copy-start(bf16[4,256,256]{2,1,0:T(8,128)(2,1)} %param.12) | copy-start | bytes 1572868
  1.0 4.7 copy-start.1
  15.0 7.6 %collective-permute-start = (f32[32,128,256]{2,0,1:T(8,128)}, f32[32,128,256]{2,0,1:T(8,128)}, u32[]{:S(2)}, u32[]{:S(2)}) collective-permute-start(f32[32,128,256]{2,0,1:T(8,128)} %fusion.8), channel_id=1, source_target_pairs={{0,4},{4,0},{8,12},{12,8},{16,20},{20,16},{24,28},{28,24},{1,5},{5... | collective-permute-start | bytes 12582920 | tf_op jit(solution)/shard_map/ppermute | solution.py:21
  29.6 94.0 %collective-permute-start.1 = (f32[32,128,256]{2,0,1:T(8,128)}, f32[32,128,256]{2,0,1:T(8,128)}, u32[]{:S(2)}, u32[]{:S(2)}) collective-permute-start(f32[32,128,256]{2,0,1:T(8,128)} %multiply_add_fusion.3), channel_id=1, source_target_pairs={{0,8},{8,0},{4,12},{12,4},{16,24},{24,16},{20,28},{28,20},{1,9},{9... | collective-permute-start | bytes 12582920 | tf_op jit(solution)/shard_map/ppermute | solution.py:21
  130.6 92.4 %collective-permute-start.2 = (f32[32,128,256]{2,0,1:T(8,128)}, f32[32,128,256]{2,0,1:T(8,128)}, u32[]{:S(2)}, u32[]{:S(2)}) collective-permute-start(f32[32,128,256]{2,0,1:T(8,128)} %multiply_add_fusion.2), channel_id=1, source_target_pairs={{0,16},{16,0},{4,20},{20,4},{8,24},{24,8},{12,28},{28,12},{1,17},{... | collective-permute-start | bytes 12582920 | tf_op jit(solution)/shard_map/ppermute | solution.py:21
  227.5 7.2 %collective-permute-start.3 = (f32[32,128,256]{2,0,1:T(8,128)S(1)}, f32[32,128,256]{2,0,1:T(8,128)S(1)}, u32[]{:S(2)}, u32[]{:S(2)}) collective-permute-start(f32[32,128,256]{2,0,1:T(8,128)S(1)} %add_multiply_fusion), channel_id=1, source_target_pairs={{0,4},{4,0},{8,12},{12,8},{16,20},{20,16},{24,28},{28,24},{1,5},{5... | collective-permute-start | bytes 12582920 | tf_op jit(solution)/shard_map/ppermute | solution.py:21
  236.2 92.7 %collective-permute-start.4 = (f32[32,128,256]{2,0,1:T(8,128)S(1)}, f32[32,128,256]{2,0,1:T(8,128)S(1)}, u32[]{:S(2)}, u32[]{:S(2)}) collective-permute-start(f32[32,128,256]{2,0,1:T(8,128)S(1)} %multiply_add_fusion.1), channel_id=1, source_target_pairs={{0,8},{8,0},{4,12},{12,4},{16,24},{24,16},{20,28},{28,20},{1,9},{9... | collective-permute-start | bytes 12582920 | tf_op jit(solution)/shard_map/ppermute | solution.py:21
  330.3 91.9 %collective-permute-start.5 = (f32[32,128,256]{2,0,1:T(8,128)S(1)}, f32[32,128,256]{2,0,1:T(8,128)S(1)}, u32[]{:S(2)}, u32[]{:S(2)}) collective-permute-start(f32[32,128,256]{2,0,1:T(8,128)S(1)} %multiply_add_fusion), channel_id=1, source_target_pairs={{0,16},{16,0},{4,20},{20,4},{8,24},{24,8},{12,28},{28,12},{1,17},{... | collective-permute-start | bytes 12582920 | tf_op jit(solution)/shard_map/ppermute | solution.py:21
  426.3 10.0 %copy-start.2 = (bf16[8192,256]{1,0:T(8,128)(2,1)S(1)}, bf16[8192,256]{1,0:T(8,128)(2,1)}, u32[]{:S(2)}) copy-start(bf16[8192,256]{1,0:T(8,128)(2,1)} %param.8) | copy-start | bytes 12582916
  439.7 5.3 copy-start.3
  439.8 97.3 %all-to-all-start = ((bf16[4,2048,256]{2,1,0:T(8,128)(2,1)}), bf16[4,2048,256]{2,1,0:T(8,128)(2,1)}, u32[]{:S(2)}, u32[]{:S(2)}) async-start(bf16[4,2048,256]{2,1,0:T(8,128)(2,1)} %bitcast.36), calls=%async_computation | async-start | bytes 8388608 | tf_op jit(solution)/shard_map/all_to_all | solution.py:65
where the time goes:
time: 588 us; the launch traced here: 582 us
  waiting for transfers between devices  469 us (80%)
  matrix products  51.8 us (9%)
  other arithmetic  24.9 us (4%)
  local copies, waits for them, and re-layouts  22.9 us (4%)
  starting transfers between devices  13.5 us (2%)
    ppermute x6, waiting for transfers between devices, swapped(): return lax.ppermute(block, axis, route)  377 us
    all_to_all x1, waiting for transfers between devices, local(): lax.all_to_all(gated, 'ch', split_axis=0, concat_axis=1, tiled=True)  91.8 us
    dot_general x1, matrix products, local(): jnp.einsum('rie,eki->rke', first_section, mix_weight, precision=high)  17.1 us
    add x4, other arithmetic, local(): spectra = factor * spectra + math.sin(angle) * partner  16.8 us
  transfers between devices with their start and end apart: 7, of which 7 were waited for; matrix products, arithmetic and copies ran while one was open for 0% of the time, Pallas kernels for 0%

commit v1 on v0

v1 whole, which is shorter than its diff:
```python
import functools
import math

import jax
import jax.numpy as jnp
import ml_dtypes
import numpy as np
from jax import lax
from jax.experimental import pallas as pl
from jax.experimental.pallas import tpu as pltpu
from jax.sharding import PartitionSpec as P

GSZ = 16
B = 256
A = 32
KMAX = 128
LANES = 128
MESH = pl.DeviceIdType.MESH
F32 = jnp.float32
BF16 = jnp.bfloat16


def cosine_table(length):
    rows = np.arange(length, dtype=np.float64)[:, None]
    cols = np.arange(length, dtype=np.float64)[None, :]
    table = np.cos(math.pi * (2.0 * cols + 1.0) * rows / (2.0 * length)) * math.sqrt(2.0 / length)
    return np.where(rows == 0.0, table * math.sqrt(0.5), table)


def split(table):
    high = table.astype(ml_dtypes.bfloat16)
    low = (table - high.astype(np.float64)).astype(ml_dtypes.bfloat16)
    return high, low


def tables():
    band_high, band_low = split(cosine_table(B)[:KMAX])
    mid_high, mid_low = split(np.kron(cosine_table(A), np.eye(8)))
    back_high, back_low = split(np.kron(cosine_table(A).T, np.eye(8)))
    return (
        np.concatenate([band_high, band_low], 0),
        np.concatenate([mid_high, mid_low, mid_high], 1),
        np.concatenate([back_high, back_low], 1),
        np.concatenate([band_high.T, band_low.T, band_high.T], 1),
    )


def dot(left, right):
    return jnp.dot(left, right, preferred_element_type=F32)


def two_parts(value):
    high = value.astype(BF16)
    return high, (value - high.astype(F32)).astype(BF16)


def butterfly(parts, levels):
    for level in range(levels):
        angle = 0.6 + 0.1 * level
        cos, sin = math.cos(angle), math.sin(angle)
        mixed = list(parts)
        for low in range(len(parts)):
            if (low >> level) % 2 == 0:
                high = low + (1 << level)
                mixed[low] = cos * parts[low] + sin * parts[high]
                mixed[high] = sin * parts[low] - cos * parts[high]
        parts = mixed
    return parts


def filter_kernel(n, nc, halves, tok, gate, gain, dgain, keep, band, mid, back, inner, out,
                  xt, gt, gn, z, snd, rcv, mxo, bck, gsd,
                  xsem, gsem, nsem, s1, r1, s2, r2, s3, r3, own3):
    me = lax.axis_index("seq")
    mc = lax.axis_index("ch")
    levels = n.bit_length() - 1
    jn = A // n
    an = A // nc

    def cut(h):
        return pl.ds(h * LANES, LANES)

    loads = {}
    for h in range(halves):
        loads["x", h] = pltpu.make_async_copy(tok.at[:, :, cut(h)], xt.at[h], xsem.at[h])
        loads["n", h] = pltpu.make_async_copy(gain.at[:, :, cut(h)], gn.at[h], nsem.at[h])
        loads["g", h] = pltpu.make_async_copy(gate.at[:, :, cut(h)], gt.at[h], gsem.at[h])
    for name in ("x", "n"):
        loads[name, 0].start()
    for h in range(1, halves):
        loads["x", h].start()
        loads["n", h].start()
    for h in range(halves):
        loads["g", h].start()

    barrier = pltpu.get_barrier_semaphore()
    for s in range(1, n):
        pl.semaphore_signal(barrier, inc=1, device_id={"seq": lax.rem(me + s, n)}, device_id_type=MESH)
    for s in range(1, nc):
        pl.semaphore_signal(barrier, inc=1, device_id={"ch": lax.rem(mc + s, nc)}, device_id_type=MESH)

    def forward(h):
        loads["x", h].wait()

        def first(a, carry):
            both = dot(band[...], xt[h, a])
            z[a] = both[:KMAX] + both[KMAX:]
            return carry

        lax.fori_loop(0, A, first, 0, unroll=4)
        loads["n", h].wait()
        keeps = keep[:, h * LANES:(h + 1) * LANES].reshape(1, 1, LANES)

        def second(kb, carry):
            start = pl.multiple_of(kb * 16, 16)
            block = z[:, pl.ds(start, 16), :]
            pieces = []
            for part in range(2):
                value = block[:, part * 8:part * 8 + 8].reshape(A * 8, LANES)
                high, low = two_parts(value)
                pieces.append(dot(mid[...], jnp.concatenate([high, high, low], 0)).reshape(A, 8, LANES))
            value = jnp.concatenate(pieces, 1)
            index = start + lax.broadcasted_iota(jnp.int32, (1, 16, LANES), 1)
            value = value * jnp.where(index < keeps, gn[h, :, pl.ds(start, 16), :], 0.0)
            snd[h, :, :, pl.ds(start, 16), :] = value.astype(BF16).reshape(n, jn, 16, LANES)
            return carry

        lax.fori_loop(0, KMAX // 16, second, 0)

    def exchange(src, dst, ssem, rsem, h):
        copies = []
        for s in range(1, n):
            to = lax.rem(me + s, n)
            copies.append(pltpu.make_async_remote_copy(
                src_ref=src.at[h, to], dst_ref=dst.at[h, me],
                send_sem=ssem.at[h, s], recv_sem=rsem.at[h, s],
                device_id={"seq": to}, device_id_type=MESH))
        return copies

    def mix(h):
        rcv[h, me] = snd[h, me]
        rows = [dgain[r:r + 1, h * LANES:(h + 1) * LANES] for r in range(n)]

        def step(i, carry):
            j = i // (KMAX // 16)
            start = pl.multiple_of(lax.rem(i, KMAX // 16) * 16, 16)
            parts = [rcv[h, p, j, pl.ds(start, 16), :].astype(F32) for p in range(n)]
            parts = butterfly(parts, levels)
            parts = [part * row for part, row in zip(parts, rows)]
            parts = butterfly(parts, levels)
            for q in range(n):
                mxo[h, q, j, pl.ds(start, 16), :] = parts[q].astype(BF16)
            return carry

        lax.fori_loop(0, jn * (KMAX // 16), step, 0)
        bck[h, me] = mxo[h, me]

    def inverse_mid(h):
        def step(kb, carry):
            start = pl.multiple_of(kb * 16, 16)
            block = bck[h, :, :, pl.ds(start, 16), :].reshape(A, 16, LANES).astype(F32)
            for part in range(2):
                value = block[:, part * 8:part * 8 + 8].reshape(A * 8, LANES).astype(BF16)
                value = dot(back[...], jnp.concatenate([value, value], 0))
                z[:, pl.ds(start + part * 8, 8), :] = value.reshape(A, 8, LANES)
            return carry

        lax.fori_loop(0, KMAX // 16, step, 0)

    def inverse_rows(h, to):
        def step(i, carry):
            a = to * an + i
            high, low = two_parts(z[a])
            smooth = dot(inner[...], jnp.concatenate([high, high, low], 0))
            gsd[h, a] = (smooth * gt[h, a].astype(F32)).astype(BF16)
            return carry

        lax.fori_loop(0, an, step, 0, unroll=2)

    def run(copies):
        for copy in copies:
            copy.start()

    first = [exchange(snd, rcv, s1, r1, h) for h in range(halves)]
    second = [exchange(mxo, bck, s2, r2, h) for h in range(halves)]
    third = []

    def finish(h):
        for copy in second[h]:
            copy.wait_recv()
        inverse_mid(h)
        loads["g", h].wait()
        for s in list(range(nc // 2, 0, -1)) + list(range(nc // 2 + 1, nc)):
            to = lax.rem(mc + s, nc)
            inverse_rows(h, to)
            copy = pltpu.make_async_remote_copy(
                src_ref=gsd.at[h, pl.ds(to * an, an)], dst_ref=out.at[h, mc],
                send_sem=s3.at[h, s], recv_sem=r3.at[h, s],
                device_id={"ch": to}, device_id_type=MESH)
            copy.start()
            third.append(copy)
        inverse_rows(h, mc)
        copy = pltpu.make_async_copy(gsd.at[h, pl.ds(mc * an, an)], out.at[h, mc], own3.at[h])
        copy.start()
        third.append(copy)

    forward(0)
    pl.semaphore_wait(barrier, n - 1 + nc - 1)
    run(first[0])
    for h in range(halves):
        if h + 1 < halves:
            forward(h + 1)
        for copy in first[h]:
            copy.wait_recv()
        mix(h)
        run(second[h])
        if h + 1 < halves:
            run(first[h + 1])
        finish(h)
    for copy in third:
        copy.wait()
    for copies in first + second:
        for copy in copies:
            copy.wait_send()


def mixing_kernel(nc, halves, nb, gathered, weight, mixing, out):
    size = weight.shape[1]
    per = size // LANES
    tiles = [gathered[h, c].reshape(-1, LANES) for c in range(nc) for h in range(halves)]
    sections = [
        dot(jnp.concatenate(tiles[i * per:(i + 1) * per], 1), weight[i]) for i in range(nb)
    ]
    for k in range(nb):
        total = sections[0] * mixing[k * nb:k * nb + 1]
        for i in range(1, nb):
            total += sections[i] * mixing[k * nb + i:k * nb + i + 1]
        out[:, k * size:(k + 1) * size] = total.astype(BF16)


def local(n, nc, tokens, gating, spectral_gain, device_gain, retained, block_weight, mix_weight):
    rows, width = tokens.shape
    halves = width // LANES
    an = A // nc
    jn = A // n
    keep = jnp.repeat(retained, GSZ)[None, :]
    any_space = pl.BlockSpec(memory_space=pl.ANY)
    vmem = pl.BlockSpec(memory_space=pltpu.VMEM)
    dma = pltpu.SemaphoreType.DMA
    share = (halves, n, jn, KMAX, LANES)
    gathered = pl.pallas_call(
        functools.partial(filter_kernel, n, nc, halves),
        out_shape=jax.ShapeDtypeStruct((halves, nc, an, B, LANES), BF16),
        in_specs=[any_space] * 3 + [vmem] * 6,
        out_specs=any_space,
        scratch_shapes=[
            pltpu.VMEM((halves, A, B, LANES), BF16),
            pltpu.VMEM((halves, A, B, LANES), BF16),
            pltpu.VMEM((halves, A, KMAX, LANES), F32),
            pltpu.VMEM((A, KMAX, LANES), F32),
            pltpu.VMEM(share, BF16),
            pltpu.VMEM(share, BF16),
            pltpu.VMEM(share, BF16),
            pltpu.VMEM(share, BF16),
            pltpu.VMEM((halves, A, B, LANES), BF16),
            dma((halves,)), dma((halves,)), dma((halves,)),
            dma((halves, n)), dma((halves, n)), dma((halves, n)), dma((halves, n)),
            dma((halves, nc)), dma((halves, nc)), dma((halves,)),
        ],
        compiler_params=pltpu.CompilerParams(
            collective_id=0, has_side_effects=True, vmem_limit_bytes=48 * 1024 * 1024),
        name="filter",
    )(tokens.reshape(A, B, width), gating.reshape(A, B, width), spectral_gain, device_gain, keep,
      *[jnp.asarray(table) for table in tables()])
    nb, size, _ = block_weight.shape
    mixing = jnp.transpose(mix_weight, (1, 2, 0)).reshape(nb * nb, size)
    step = 2 if an % 2 == 0 else 1
    return pl.pallas_call(
        functools.partial(mixing_kernel, nc, halves, nb),
        out_shape=jax.ShapeDtypeStruct((an * B, nb * size), BF16),
        grid=(an // step,),
        in_specs=[
            pl.BlockSpec((halves, nc, step, B, LANES), lambda i: (0, 0, i, 0, 0)),
            pl.BlockSpec(block_weight.shape, lambda i: (0, 0, 0)),
            pl.BlockSpec(mixing.shape, lambda i: (0, 0)),
        ],
        out_specs=pl.BlockSpec((step * B, nb * size), lambda i: (i, 0)),
        compiler_params=pltpu.CompilerParams(vmem_limit_bytes=40 * 1024 * 1024),
        name="mixing",
    )(gathered, block_weight, mixing)


def solution(mesh):
    in_specs = (
        P("seq", "ch"),
        P("seq", "ch"),
        P(None, None, "ch"),
        P(None, "ch"),
        P("ch"),
        P(),
        P(),
    )
    out_specs = P(("seq", "ch"), None)
    body = functools.partial(local, mesh.shape["seq"], mesh.shape["ch"])
    return jax.shard_map(body, mesh=mesh, in_specs=in_specs, out_specs=out_specs, check_vma=False)
```

time: 588 us -> 141 us (0.24)
  the two profiles are of different devices: /device:TPU:0 before, /device:TPU:9 now
where the time goes in v1:
time: 141 us; the launch traced here: 140 us
  Pallas kernels  134 us (95%)
  local copies, waits for them, and re-layouts  6.01 us (4%)
    pallas_call x1, Pallas kernels, local(): pl.pallas_call(functools.partial(filter_kernel, n, nc, halves), out_shape...  130 us
    unnamed x12, local copies, waits for them, and re-layouts  4.47 us
    pallas_call x1, Pallas kernels, local(): pl.pallas_call(functools.partial(mixing_kernel, nc, halves, nb), out_shap...  4.37 us

profile of v1, /device:TPU:9, one launch (start us, length us, event | category | flops | bytes accessed | tf_op | source)
XLA Modules:
  0.0 140.4 jit_solution(5860798253913376426)
XLA Ops:
  0.0 0.7 broadcast_in_dim.3
  0.7 0.1 broadcast_in_dim_reshape.3.keep
  0.8 0.7 reshape.11.mixing
  1.5 0.0 copy-start.1
  1.5 1.0 copy-done.1
  2.5 0.0 copy-start.2
  2.5 0.9 copy-done.2
  3.5 0.0 copy-start.3
  3.5 0.9 copy-done.3
  4.4 0.0 copy-start.4
  4.4 0.9 copy-done.4
  5.3 0.0 copy-start.5
  5.3 0.7 copy-done.5
  6.0 0.0 copy-start
  6.0 130.0 %filter.1.gathered = bf16[2,4,8,256,128]{4,3,2,1,0:T(8,128)(2,1)S(1)} custom-call(bf16[32,256,256]{2,1,0:T(8,128)(2,1)} %bitcast.3, bf16[32,256,256]{2,1,0:T(8,128)(2,1)} %bitcast.4, f32[32,128,256]{2,1,0:T(8,128)} %gain.1, f32[8,256]{1,0:T(8,128)S(1)} %copy-done.5, s32[1,256]{1,0:T(1,128)S(1)} %broadcast_in_dim_reshape.3.keep, ...), custom_call_target="tpu_custom_call" | custom-call | tf_op jit(solution)/shard_map/filter/pallas_call | solution.py:251
  136.0 0.0 copy-done
  136.0 4.4 %mixing.1 = bf16[2048,1024]{1,0:T(8,128)(2,1)} custom-call(bf16[2,4,8,256,128]{4,3,2,1,0:T(8,128)(2,1)S(1)} %filter.1.gathered, bf16[4,256,256]{2,1,0:T(8,128)(2,1)S(1)} %copy-done, f32[16,256]{1,0:T(8,128)S(1)} %reshape.11.mixing), custom_call_target="tpu_custom_call" | custom-call | tf_op jit(solution)/shard_map/mixing/pallas_call | solution.py:278
Async XLA Ops:
  1.5 1.0 copy-start.1
  2.5 0.9 copy-start.2
  3.5 0.9 copy-start.3
  4.4 0.9 copy-start.4
  5.3 0.7 copy-start.5
  6.0 130.0 %copy-start = (bf16[4,256,256]{2,1,0:T(8,128)(2,1)S(1)}, bf16[4,256,256]{2,1,0:T(8,128)(2,1)}, u32[]{:S(2)}) copy-start(bf16[4,256,256]{2,1,0:T(8,128)(2,1)} %weight.1) | copy-start | bytes 1572868

commit v2 on v1

--- a/solution.py
+++ b/solution.py
@@ -68,9 +68,11 @@
     return parts
 
 
-def filter_kernel(n, nc, halves, tok, gate, gain, dgain, keep, band, mid, back, inner, out,
-                  xt, gt, gn, z, snd, rcv, mxo, bck, gsd,
-                  xsem, gsem, nsem, s1, r1, s2, r2, s3, r3, own3):
+def filter_kernel(n, nc, halves, early, tok, gate, gain, dgain, kept,
+                  band_hbm, mid_hbm, back_hbm, inner_hbm, out,
+                  xt, gt, gn, z, snd, rcv, mxo, bck, gsd, ysd, yrc, grc, ystage,
+                  band, mid, back, inner, dg, retained, tsem,
+                  xsem, gsem, nsem, s1, r1, s2, r2, s3, r3, own3, s4, r4, s5, r5, own5):
     me = lax.axis_index("seq")
     mc = lax.axis_index("ch")
     levels = n.bit_length() - 1
@@ -85,8 +87,17 @@
         loads["x", h] = pltpu.make_async_copy(tok.at[:, :, cut(h)], xt.at[h], xsem.at[h])
         loads["n", h] = pltpu.make_async_copy(gain.at[:, :, cut(h)], gn.at[h], nsem.at[h])
         loads["g", h] = pltpu.make_async_copy(gate.at[:, :, cut(h)], gt.at[h], gsem.at[h])
-    for name in ("x", "n"):
-        loads[name, 0].start()
+    for i, (src, dst) in enumerate((
+            (band_hbm, band), (mid_hbm, mid), (dgain, dg), (back_hbm, back), (inner_hbm, inner),
+            (kept, retained))):
+        loads["t", i] = pltpu.make_async_copy(src, dst, tsem.at[i])
+    loads["t", 5].start()
+    loads["t", 0].start()
+    loads["x", 0].start()
+    loads["t", 1].start()
+    loads["n", 0].start()
+    for i in (2, 3, 4):
+        loads["t", i].start()
     for h in range(1, halves):
         loads["x", h].start()
         loads["n", h].start()
@@ -101,6 +112,8 @@
 
     def forward(h):
         loads["x", h].wait()
+        if h == 0:
+            loads["t", 0].wait()
 
         def first(a, carry):
             both = dot(band[...], xt[h, a])
@@ -109,7 +122,13 @@
 
         lax.fori_loop(0, A, first, 0, unroll=4)
         loads["n", h].wait()
-        keeps = keep[:, h * LANES:(h + 1) * LANES].reshape(1, 1, LANES)
+        if h == 0:
+            loads["t", 1].wait()
+            loads["t", 5].wait()
+        group = lax.broadcasted_iota(jnp.int32, (1, 1, LANES), 2) // GSZ
+        keeps = jnp.zeros((1, 1, LANES), jnp.int32)
+        for i in range(LANES // GSZ):
+            keeps = jnp.where(group == i, retained[h * (LANES // GSZ) + i], keeps)
 
         def second(kb, carry):
             start = pl.multiple_of(kb * 16, 16)
@@ -139,7 +158,10 @@
 
     def mix(h):
         rcv[h, me] = snd[h, me]
-        rows = [dgain[r:r + 1, h * LANES:(h + 1) * LANES] for r in range(n)]
+        if h == 0:
+            for i in (2, 3, 4):
+                loads["t", i].wait()
+        rows = [dg[r:r + 1, h * LANES:(h + 1) * LANES] for r in range(n)]
 
         def step(i, carry):
             j = i // (KMAX // 16)
@@ -167,7 +189,7 @@
 
         lax.fori_loop(0, KMAX // 16, step, 0)
 
-    def inverse_rows(h, to):
+    def inverse_rows(h, to, skip):
         def step(i, carry):
             a = to * an + i
             high, low = two_parts(z[a])
@@ -175,7 +197,7 @@
             gsd[h, a] = (smooth * gt[h, a].astype(F32)).astype(BF16)
             return carry
 
-        lax.fori_loop(0, an, step, 0, unroll=2)
+        lax.fori_loop(skip, an, step, 0)
 
     def run(copies):
         for copy in copies:
@@ -184,28 +206,51 @@
     first = [exchange(snd, rcv, s1, r1, h) for h in range(halves)]
     second = [exchange(mxo, bck, s2, r2, h) for h in range(halves)]
     third = []
+    fourth = []
+    order = list(range(nc // 2, 0, -1)) + list(range(nc // 2 + 1, nc))
 
     def finish(h):
         for copy in second[h]:
             copy.wait_recv()
         inverse_mid(h)
         loads["g", h].wait()
-        for s in list(range(nc // 2, 0, -1)) + list(range(nc // 2 + 1, nc)):
+        skip = early if h == 0 else 0
+        if h == 0:
+            for s in order:
+                to = lax.rem(mc + s, nc)
+                ysd[pl.ds(to * early, early)] = z[pl.ds(to * an, early)].astype(BF16)
+                copy = pltpu.make_async_remote_copy(
+                    src_ref=ysd.at[pl.ds(to * early, early)], dst_ref=yrc.at[s],
+                    send_sem=s5.at[s], recv_sem=r5.at[s],
+                    device_id={"ch": to}, device_id_type=MESH)
+                copy.start()
+                fourth.append((s, copy))
+        for s in order:
             to = lax.rem(mc + s, nc)
-            inverse_rows(h, to)
+            inverse_rows(h, to, skip)
             copy = pltpu.make_async_remote_copy(
-                src_ref=gsd.at[h, pl.ds(to * an, an)], dst_ref=out.at[h, mc],
+                src_ref=gsd.at[h, pl.ds(to * an + skip, an - skip)],
+                dst_ref=out.at[h, mc, pl.ds(skip, an - skip)],
                 send_sem=s3.at[h, s], recv_sem=r3.at[h, s],
                 device_id={"ch": to}, device_id_type=MESH)
             copy.start()
             third.append(copy)
-        inverse_rows(h, mc)
+        inverse_rows(h, mc, 0)
         copy = pltpu.make_async_copy(gsd.at[h, pl.ds(mc * an, an)], out.at[h, mc], own3.at[h])
         copy.start()
         third.append(copy)
 
+    pl.semaphore_wait(barrier, n - 1 + nc - 1)
+    gates = []
+    for s in order:
+        to = lax.rem(mc + s, nc)
+        copy = pltpu.make_async_remote_copy(
+            src_ref=gate.at[pl.ds(to * an, early), :, cut(0)], dst_ref=grc.at[s],
+            send_sem=s4.at[s], recv_sem=r4.at[s],
+            device_id={"ch": to}, device_id_type=MESH)
+        copy.start()
+        gates.append(copy)
     forward(0)
-    pl.semaphore_wait(barrier, n - 1 + nc - 1)
     run(first[0])
     for h in range(halves):
         if h + 1 < halves:
@@ -217,7 +262,24 @@
         if h + 1 < halves:
             run(first[h + 1])
         finish(h)
-    for copy in third:
+    stores = []
+    for copy in gates:
+        copy.wait()
+    for s, copy in fourth:
+        copy.wait()
+
+        def step(a, carry):
+            value = yrc[s, a]
+            smooth = dot(inner[:, :2 * KMAX], jnp.concatenate([value, value], 0))
+            ystage[s, a] = (smooth * grc[s, a].astype(F32)).astype(BF16)
+            return carry
+
+        lax.fori_loop(0, early, step, 0)
+        source = lax.rem(mc + nc - s, nc)
+        store = pltpu.make_async_copy(ystage.at[s], out.at[0, source, pl.ds(0, early)], own5.at[s])
+        store.start()
+        stores.append(store)
+    for copy in stores + third:
         copy.wait()
     for copies in first + second:
         for copy in copies:
@@ -243,15 +305,15 @@
     halves = width // LANES
     an = A // nc
     jn = A // n
-    keep = jnp.repeat(retained, GSZ)[None, :]
+    early = max(1, an * 5 // 8)
+    steps = [jnp.asarray(table) for table in tables()]
     any_space = pl.BlockSpec(memory_space=pl.ANY)
-    vmem = pl.BlockSpec(memory_space=pltpu.VMEM)
     dma = pltpu.SemaphoreType.DMA
     share = (halves, n, jn, KMAX, LANES)
     gathered = pl.pallas_call(
-        functools.partial(filter_kernel, n, nc, halves),
+        functools.partial(filter_kernel, n, nc, halves, early),
         out_shape=jax.ShapeDtypeStruct((halves, nc, an, B, LANES), BF16),
-        in_specs=[any_space] * 3 + [vmem] * 6,
+        in_specs=[pl.BlockSpec(memory_space=pltpu.HBM)] * 9,
         out_specs=any_space,
         scratch_shapes=[
             pltpu.VMEM((halves, A, B, LANES), BF16),
@@ -263,15 +325,24 @@
             pltpu.VMEM(share, BF16),
             pltpu.VMEM(share, BF16),
             pltpu.VMEM((halves, A, B, LANES), BF16),
+            pltpu.VMEM((nc * early, KMAX, LANES), BF16),
+            pltpu.VMEM((nc, early, KMAX, LANES), BF16),
+            pltpu.VMEM((nc, early, B, LANES), BF16),
+            pltpu.VMEM((nc, early, B, LANES), BF16),
+            *[pltpu.VMEM(step.shape, BF16) for step in steps],
+            pltpu.VMEM((n, width), F32),
+            pltpu.SMEM((LANES,), jnp.int32),
+            dma((6,)),
             dma((halves,)), dma((halves,)), dma((halves,)),
             dma((halves, n)), dma((halves, n)), dma((halves, n)), dma((halves, n)),
             dma((halves, nc)), dma((halves, nc)), dma((halves,)),
+            dma((nc,)), dma((nc,)), dma((nc,)), dma((nc,)), dma((nc,)),
         ],
         compiler_params=pltpu.CompilerParams(
-            collective_id=0, has_side_effects=True, vmem_limit_bytes=48 * 1024 * 1024),
+            collective_id=0, has_side_effects=True, vmem_limit_bytes=60 * 1024 * 1024),
         name="filter",
-    )(tokens.reshape(A, B, width), gating.reshape(A, B, width), spectral_gain, device_gain, keep,
-      *[jnp.asarray(table) for table in tables()])
+    )(tokens.reshape(A, B, width), gating.reshape(A, B, width), spectral_gain, device_gain,
+      jnp.pad(retained, (0, LANES - retained.shape[0])), *steps)
     nb, size, _ = block_weight.shape
     mixing = jnp.transpose(mix_weight, (1, 2, 0)).reshape(nb * nb, size)
     step = 2 if an % 2 == 0 else 1
@@ -285,7 +356,7 @@
             pl.BlockSpec(mixing.shape, lambda i: (0, 0)),
         ],
         out_specs=pl.BlockSpec((step * B, nb * size), lambda i: (i, 0)),
-        compiler_params=pltpu.CompilerParams(vmem_limit_bytes=40 * 1024 * 1024),
+        compiler_params=pltpu.CompilerParams(vmem_limit_bytes=60 * 1024 * 1024),
         name="mixing",
     )(gathered, block_weight, mixing)
 

time: 141 us -> 125 us (0.89)
  Pallas kernels: 134 us -> 122 us
  local copies, waits for them, and re-layouts: 6.01 us -> 2.49 us
    pallas_call x1, Pallas kernels: 130 us -> 116 us  [local(): pl.pallas_call(functools.partial(filter_kernel, n, nc, halves, early), ou...]
    unnamed x12 -> x0, local copies, waits for them, and re-layouts: 4.47 us -> none
    pallas_call x1, Pallas kernels: 4.37 us -> 6.25 us  [local(): pl.pallas_call(functools.partial(mixing_kernel, nc, halves, nb), out_shap...]
where the time goes in v2:
time: 125 us; the launch traced here: 124 us
  Pallas kernels  122 us (98%)
  local copies, waits for them, and re-layouts  2.49 us (2%)
    pallas_call x1, Pallas kernels, local(): pl.pallas_call(functools.partial(filter_kernel, n, nc, halves, early), ou...  116 us
    pallas_call x1, Pallas kernels, local(): pl.pallas_call(functools.partial(mixing_kernel, nc, halves, nb), out_shap...  6.25 us

profile of v2, /device:TPU:9, one launch (start us, length us, event | category | flops | bytes accessed | tf_op | source)
XLA Modules:
  0.0 124.3 jit_solution(5344434439085413748)
XLA Ops:
  0.0 1.2 pad.4.kept
  1.2 1.3 %reshape.11.mixing = f32[16,256]{1,0:T(8,128)} reshape(f32[4,4,256]{2,1,0:T(4,128)} %bitcast.5) | data formatting | bytes 32768 | tf_op jit(solution)/shard_map/reshape | solution.py:347
  2.5 115.5 %filter.1.gathered = bf16[2,4,8,256,128]{4,3,2,1,0:T(8,128)(2,1)} custom-call(bf16[32,256,256]{2,1,0:T(8,128)(2,1)} %bitcast.3, bf16[32,256,256]{2,1,0:T(8,128)(2,1)} %bitcast.4, f32[32,128,256]{2,1,0:T(8,128)} %gain.1, f32[8,256]{1,0:T(8,128)} %dgain.1, s32[128]{0:T(128)} %pad.4.kept, bf16[256,256]{1,0:T(8,128)(2,1)} %constant.10.clone.band_hbm, ...), custom_call_target="tpu_custom_call" | custom-call | tf_op jit(solution)/shard_map/filter/pallas_call | solution.py:313
  118.0 6.2 %mixing.1 = bf16[2048,1024]{1,0:T(8,128)(2,1)} custom-call(bf16[2,4,8,256,128]{4,3,2,1,0:T(8,128)(2,1)} %filter.1.gathered, bf16[4,256,256]{2,1,0:T(8,128)(2,1)} %weight.1, f32[16,256]{1,0:T(8,128)} %reshape.11.mixing), custom_call_target="tpu_custom_call" | custom-call | tf_op jit(solution)/shard_map/mixing/pallas_call | solution.py:349

commit v3 on v2

--- a/solution.py
+++ b/solution.py
@@ -115,12 +115,15 @@
         if h == 0:
             loads["t", 0].wait()
 
-        def first(a, carry):
-            both = dot(band[...], xt[h, a])
-            z[a] = both[:KMAX] + both[KMAX:]
-            return carry
-
-        lax.fori_loop(0, A, first, 0, unroll=4)
+        def first(i, carry):
+            a = i * 2
+            both = dot(band[...], jnp.concatenate([xt[h, a], xt[h, a + 1]], 1))
+            both = both[:KMAX] + both[KMAX:]
+            z[a] = both[:, :LANES]
+            z[a + 1] = both[:, LANES:]
+            return carry
+
+        lax.fori_loop(0, A // 2, first, 0, unroll=4)
         loads["n", h].wait()
         if h == 0:
             loads["t", 1].wait()
@@ -137,7 +140,9 @@
             for part in range(2):
                 value = block[:, part * 8:part * 8 + 8].reshape(A * 8, LANES)
                 high, low = two_parts(value)
-                pieces.append(dot(mid[...], jnp.concatenate([high, high, low], 0)).reshape(A, 8, LANES))
+                pieces.append(jnp.concatenate([high, high, low], 0))
+            value = dot(mid[...], jnp.concatenate(pieces, 1))
+            pieces = [value[:, i * LANES:(i + 1) * LANES].reshape(A, 8, LANES) for i in range(2)]
             value = jnp.concatenate(pieces, 1)
             index = start + lax.broadcasted_iota(jnp.int32, (1, 16, LANES), 1)
             value = value * jnp.where(index < keeps, gn[h, :, pl.ds(start, 16), :], 0.0)
@@ -181,23 +186,26 @@
         def step(kb, carry):
             start = pl.multiple_of(kb * 16, 16)
             block = bck[h, :, :, pl.ds(start, 16), :].reshape(A, 16, LANES).astype(F32)
-            for part in range(2):
-                value = block[:, part * 8:part * 8 + 8].reshape(A * 8, LANES).astype(BF16)
-                value = dot(back[...], jnp.concatenate([value, value], 0))
-                z[:, pl.ds(start + part * 8, 8), :] = value.reshape(A, 8, LANES)
+            pieces = [block[:, i * 8:i * 8 + 8].reshape(A * 8, LANES).astype(BF16) for i in range(2)]
+            value = jnp.concatenate(pieces, 1)
+            value = dot(back[...], jnp.concatenate([value, value], 0))
+            for i in range(2):
+                part = value[:, i * LANES:(i + 1) * LANES]
+                z[:, pl.ds(start + i * 8, 8), :] = part.reshape(A, 8, LANES)
             return carry
 
         lax.fori_loop(0, KMAX // 16, step, 0)
 
     def inverse_rows(h, to, skip):
         def step(i, carry):
-            a = to * an + i
-            high, low = two_parts(z[a])
+            a = to * an + skip + i * 2
+            high, low = two_parts(jnp.concatenate([z[a], z[a + 1]], 1))
             smooth = dot(inner[...], jnp.concatenate([high, high, low], 0))
-            gsd[h, a] = (smooth * gt[h, a].astype(F32)).astype(BF16)
-            return carry
-
-        lax.fori_loop(skip, an, step, 0)
+            gsd[h, a] = (smooth[:, :LANES] * gt[h, a].astype(F32)).astype(BF16)
+            gsd[h, a + 1] = (smooth[:, LANES:] * gt[h, a + 1].astype(F32)).astype(BF16)
+            return carry
+
+        lax.fori_loop(0, (an - skip) // 2, step, 0)
 
     def run(copies):
         for copy in copies:
@@ -207,7 +215,15 @@
     second = [exchange(mxo, bck, s2, r2, h) for h in range(halves)]
     third = []
     fourth = []
-    order = list(range(nc // 2, 0, -1)) + list(range(nc // 2 + 1, nc))
+    order = [s for level in reversed(range(nc.bit_length() - 1)) for s in range(1 << level, 2 << level)]
+
+    def partner(s):
+        to = mc
+        for level in range(nc.bit_length() - 1):
+            if (s >> level) % 2:
+                to = to + (1 << level) - lax.rem(mc // (1 << level), 2) * (2 << level)
+        return to
+
 
     def finish(h):
         for copy in second[h]:
@@ -217,7 +233,7 @@
         skip = early if h == 0 else 0
         if h == 0:
             for s in order:
-                to = lax.rem(mc + s, nc)
+                to = partner(s)
                 ysd[pl.ds(to * early, early)] = z[pl.ds(to * an, early)].astype(BF16)
                 copy = pltpu.make_async_remote_copy(
                     src_ref=ysd.at[pl.ds(to * early, early)], dst_ref=yrc.at[s],
@@ -226,7 +242,7 @@
                 copy.start()
                 fourth.append((s, copy))
         for s in order:
-            to = lax.rem(mc + s, nc)
+            to = partner(s)
             inverse_rows(h, to, skip)
             copy = pltpu.make_async_remote_copy(
                 src_ref=gsd.at[h, pl.ds(to * an + skip, an - skip)],
@@ -243,7 +259,7 @@
     pl.semaphore_wait(barrier, n - 1 + nc - 1)
     gates = []
     for s in order:
-        to = lax.rem(mc + s, nc)
+        to = partner(s)
         copy = pltpu.make_async_remote_copy(
             src_ref=gate.at[pl.ds(to * an, early), :, cut(0)], dst_ref=grc.at[s],
             send_sem=s4.at[s], recv_sem=r4.at[s],
@@ -268,14 +284,16 @@
     for s, copy in fourth:
         copy.wait()
 
-        def step(a, carry):
-            value = yrc[s, a]
+        def step(i, carry):
+            a = i * 2
+            value = jnp.concatenate([yrc[s, a], yrc[s, a + 1]], 1)
             smooth = dot(inner[:, :2 * KMAX], jnp.concatenate([value, value], 0))
-            ystage[s, a] = (smooth * grc[s, a].astype(F32)).astype(BF16)
-            return carry
-
-        lax.fori_loop(0, early, step, 0)
-        source = lax.rem(mc + nc - s, nc)
+            ystage[s, a] = (smooth[:, :LANES] * grc[s, a].astype(F32)).astype(BF16)
+            ystage[s, a + 1] = (smooth[:, LANES:] * grc[s, a + 1].astype(F32)).astype(BF16)
+            return carry
+
+        lax.fori_loop(0, early // 2, step, 0)
+        source = partner(s)
         store = pltpu.make_async_copy(ystage.at[s], out.at[0, source, pl.ds(0, early)], own5.at[s])
         store.start()
         stores.append(store)
@@ -294,9 +312,9 @@
         dot(jnp.concatenate(tiles[i * per:(i + 1) * per], 1), weight[i]) for i in range(nb)
     ]
     for k in range(nb):
-        total = sections[0] * mixing[k * nb:k * nb + 1]
+        total = sections[0] * mixing[k, 0:1]
         for i in range(1, nb):
-            total += sections[i] * mixing[k * nb + i:k * nb + i + 1]
+            total += sections[i] * mixing[k, i:i + 1]
         out[:, k * size:(k + 1) * size] = total.astype(BF16)
 
 
@@ -305,7 +323,7 @@
     halves = width // LANES
     an = A // nc
     jn = A // n
-    early = max(1, an * 5 // 8)
+    early = max(2, an * 3 // 8 * 2)
     steps = [jnp.asarray(table) for table in tables()]
     any_space = pl.BlockSpec(memory_space=pl.ANY)
     dma = pltpu.SemaphoreType.DMA
@@ -331,7 +349,7 @@
             pltpu.VMEM((nc, early, B, LANES), BF16),
             *[pltpu.VMEM(step.shape, BF16) for step in steps],
             pltpu.VMEM((n, width), F32),
-            pltpu.SMEM((LANES,), jnp.int32),
+            pltpu.SMEM(retained.shape, jnp.int32),
             dma((6,)),
             dma((halves,)), dma((halves,)), dma((halves,)),
             dma((halves, n)), dma((halves, n)), dma((halves, n)), dma((halves, n)),
@@ -342,10 +360,10 @@
             collective_id=0, has_side_effects=True, vmem_limit_bytes=60 * 1024 * 1024),
         name="filter",
     )(tokens.reshape(A, B, width), gating.reshape(A, B, width), spectral_gain, device_gain,
-      jnp.pad(retained, (0, LANES - retained.shape[0])), *steps)
+      retained, *steps)
     nb, size, _ = block_weight.shape
-    mixing = jnp.transpose(mix_weight, (1, 2, 0)).reshape(nb * nb, size)
-    step = 2 if an % 2 == 0 else 1
+    mixing = jnp.transpose(mix_weight, (1, 2, 0))
+    step = 1
     return pl.pallas_call(
         functools.partial(mixing_kernel, nc, halves, nb),
         out_shape=jax.ShapeDtypeStruct((an * B, nb * size), BF16),
@@ -353,7 +371,7 @@
         in_specs=[
             pl.BlockSpec((halves, nc, step, B, LANES), lambda i: (0, 0, i, 0, 0)),
             pl.BlockSpec(block_weight.shape, lambda i: (0, 0, 0)),
-            pl.BlockSpec(mixing.shape, lambda i: (0, 0)),
+            pl.BlockSpec(mixing.shape, lambda i: (0, 0, 0)),
         ],
         out_specs=pl.BlockSpec((step * B, nb * size), lambda i: (i, 0)),
         compiler_params=pltpu.CompilerParams(vmem_limit_bytes=60 * 1024 * 1024),

time: 125 us -> 122 us (0.976)
  local copies, waits for them, and re-layouts: 2.49 us -> 0 us
    pallas_call x1, Pallas kernels: 116 us -> 113 us  [local(): pl.pallas_call(functools.partial(filter_kernel, n, nc, halves, early), ou...]
    pallas_call x1, Pallas kernels: 6.25 us -> 8.25 us  [local(): pl.pallas_call(functools.partial(mixing_kernel, nc, halves, nb), out_shap...]
    reshape x1 -> x0, local copies, waits for them, and re-layouts: 1.32 us -> none  [local(): mixing = jnp.transpose(mix_weight, (1, 2, 0)).reshape(nb * nb, size)]
where the time goes in v3:
time: 122 us; the launch traced here: 121 us
  Pallas kernels  121 us (99%)
    pallas_call x1, Pallas kernels, local(): pl.pallas_call(functools.partial(filter_kernel, n, nc, halves, early), ou...  113 us
    pallas_call x1, Pallas kernels, local(): pl.pallas_call(functools.partial(mixing_kernel, nc, halves, nb), out_shap...  8.25 us

profile of v3, /device:TPU:9, one launch (start us, length us, event | category | flops | bytes accessed | tf_op | source)
XLA Modules:
  0.0 121.3 jit_solution(10308574913854538121)
XLA Ops:
  0.0 113.1 %filter.1.gathered = bf16[2,4,8,256,128]{4,3,2,1,0:T(8,128)(2,1)} custom-call(bf16[32,256,256]{2,1,0:T(8,128)(2,1)} %bitcast.3, bf16[32,256,256]{2,1,0:T(8,128)(2,1)} %bitcast.4, f32[32,128,256]{2,1,0:T(8,128)} %gain.1, f32[8,256]{1,0:T(8,128)} %dgain.1, s32[16]{0:T(128)} %kept.1, bf16[256,256]{1,0:T(8,128)(2,1)} %constant.8.clone.band_hbm, ...), custom_call_target="tpu_custom_call" | custom-call | tf_op jit(solution)/shard_map/filter/pallas_call | solution.py:331
  113.1 8.2 %mixing.1 = bf16[2048,1024]{1,0:T(8,128)(2,1)} custom-call(bf16[2,4,8,256,128]{4,3,2,1,0:T(8,128)(2,1)} %filter.1.gathered, bf16[4,256,256]{2,1,0:T(8,128)(2,1)} %weight.1, f32[4,4,256]{2,1,0:T(4,128)} %bitcast.5), custom_call_target="tpu_custom_call" | custom-call | tf_op jit(solution)/shard_map/mixing/pallas_call | solution.py:367

commit v4 on v3

--- a/solution.py
+++ b/solution.py
@@ -215,13 +215,16 @@
     second = [exchange(mxo, bck, s2, r2, h) for h in range(halves)]
     third = []
     fourth = []
-    order = [s for level in reversed(range(nc.bit_length() - 1)) for s in range(1 << level, 2 << level)]
+    crossing = [s for level in reversed(range(nc.bit_length() - 1)) for s in range(1 << level, 2 << level)]
+
+    outer = 1 - lax.rem((mc + nc // 4) // (nc // 2), 2)
+    order = [s + outer * (i + 1 - s) for i, s in enumerate(crossing)]
 
     def partner(s):
         to = mc
         for level in range(nc.bit_length() - 1):
-            if (s >> level) % 2:
-                to = to + (1 << level) - lax.rem(mc // (1 << level), 2) * (2 << level)
+            flip = lax.rem(s // (1 << level), 2)
+            to = to + flip * ((1 << level) - lax.rem(mc // (1 << level), 2) * (2 << level))
         return to
 
 
@@ -363,7 +366,7 @@
       retained, *steps)
     nb, size, _ = block_weight.shape
     mixing = jnp.transpose(mix_weight, (1, 2, 0))
-    step = 1
+    step = 2 if an % 2 == 0 else 1
     return pl.pallas_call(
         functools.partial(mixing_kernel, nc, halves, nb),
         out_shape=jax.ShapeDtypeStruct((an * B, nb * size), BF16),

time: 122 us -> 120 us (0.984)
    pallas_call x1, Pallas kernels: 8.25 us -> 6.26 us  [local(): pl.pallas_call(functools.partial(mixing_kernel, nc, halves, nb), out_shap...]
where the time goes in v4:
time: 120 us
  Pallas kernels  120 us (100%)
    pallas_call x1, Pallas kernels, local(): pl.pallas_call(functools.partial(filter_kernel, n, nc, halves, early), ou...  113 us
    pallas_call x1, Pallas kernels, local(): pl.pallas_call(functools.partial(mixing_kernel, nc, halves, nb), out_shap...  6.26 us

profile of v4, /device:TPU:9, one launch (start us, length us, event | category | flops | bytes accessed | tf_op | source)
XLA Modules:
  0.0 119.6 jit_solution(6591281660171657436)
XLA Ops:
  0.0 113.3 %filter.1.gathered = bf16[2,4,8,256,128]{4,3,2,1,0:T(8,128)(2,1)} custom-call(bf16[32,256,256]{2,1,0:T(8,128)(2,1)} %bitcast.3, bf16[32,256,256]{2,1,0:T(8,128)(2,1)} %bitcast.4, f32[32,128,256]{2,1,0:T(8,128)} %gain.1, f32[8,256]{1,0:T(8,128)} %dgain.1, s32[16]{0:T(128)} %kept.1, bf16[256,256]{1,0:T(8,128)(2,1)} %constant.8.clone.band_hbm, ...), custom_call_target="tpu_custom_call" | custom-call | tf_op jit(solution)/shard_map/filter/pallas_call | solution.py:334
  113.3 6.3 %mixing.1 = bf16[2048,1024]{1,0:T(8,128)(2,1)} custom-call(bf16[2,4,8,256,128]{4,3,2,1,0:T(8,128)(2,1)} %filter.1.gathered, bf16[4,256,256]{2,1,0:T(8,128)(2,1)} %weight.1, f32[4,4,256]{2,1,0:T(4,128)} %bitcast.5), custom_call_target="tpu_custom_call" | custom-call | tf_op jit(solution)/shard_map/mixing/pallas_call | solution.py:370

commit v5 on v4

--- a/solution.py
+++ b/solution.py
@@ -206,6 +206,11 @@
             return carry
 
         lax.fori_loop(0, (an - skip) // 2, step, 0)
+        if (an - skip) % 2:
+            a = to * an + an - 1
+            high, low = two_parts(z[a])
+            smooth = dot(inner[...], jnp.concatenate([high, high, low], 0))
+            gsd[h, a] = (smooth * gt[h, a].astype(F32)).astype(BF16)
 
     def run(copies):
         for copy in copies:
@@ -296,6 +301,11 @@
             return carry
 
         lax.fori_loop(0, early // 2, step, 0)
+        if early % 2:
+            a = early - 1
+            value = yrc[s, a]
+            smooth = dot(inner[:, :2 * KMAX], jnp.concatenate([value, value], 0))
+            ystage[s, a] = (smooth * grc[s, a].astype(F32)).astype(BF16)
         source = partner(s)
         store = pltpu.make_async_copy(ystage.at[s], out.at[0, source, pl.ds(0, early)], own5.at[s])
         store.start()
@@ -326,7 +336,7 @@
     halves = width // LANES
     an = A // nc
     jn = A // n
-    early = max(2, an * 3 // 8 * 2)
+    early = max(1, an * 5 // 8)
     steps = [jnp.asarray(table) for table in tables()]
     any_space = pl.BlockSpec(memory_space=pl.ANY)
     dma = pltpu.SemaphoreType.DMA
@@ -366,7 +376,7 @@
       retained, *steps)
     nb, size, _ = block_weight.shape
     mixing = jnp.transpose(mix_weight, (1, 2, 0))
-    step = 2 if an % 2 == 0 else 1
+    step = 4 if an % 4 == 0 else 1
     return pl.pallas_call(
         functools.partial(mixing_kernel, nc, halves, nb),
         out_shape=jax.ShapeDtypeStruct((an * B, nb * size), BF16),

time: 120 us -> 120 us (level)
  no operation moved by 1% of the time
where the time goes in v5:
time: 120 us; the launch traced here: 119 us
  Pallas kernels  119 us (99%)
    pallas_call x1, Pallas kernels, local(): pl.pallas_call(functools.partial(filter_kernel, n, nc, halves, early), ou...  114 us
    pallas_call x1, Pallas kernels, local(): pl.pallas_call(functools.partial(mixing_kernel, nc, halves, nb), out_shap...  5.7 us

profile of v5, /device:TPU:9, one launch (start us, length us, event | category | flops | bytes accessed | tf_op | source)
XLA Modules:
  0.0 119.4 jit_solution(1811670636220531801)
XLA Ops:
  0.0 113.7 %filter.1.gathered = bf16[2,4,8,256,128]{4,3,2,1,0:T(8,128)(2,1)} custom-call(bf16[32,256,256]{2,1,0:T(8,128)(2,1)} %bitcast.3, bf16[32,256,256]{2,1,0:T(8,128)(2,1)} %bitcast.4, f32[32,128,256]{2,1,0:T(8,128)} %gain.1, f32[8,256]{1,0:T(8,128)} %dgain.1, s32[16]{0:T(128)} %kept.1, bf16[256,256]{1,0:T(8,128)(2,1)} %constant.8.clone.band_hbm, ...), custom_call_target="tpu_custom_call" | custom-call | tf_op jit(solution)/shard_map/filter/pallas_call | solution.py:344
  113.7 5.7 %mixing.1 = bf16[2048,1024]{1,0:T(8,128)(2,1)} custom-call(bf16[2,4,8,256,128]{4,3,2,1,0:T(8,128)(2,1)} %filter.1.gathered, bf16[4,256,256]{2,1,0:T(8,128)(2,1)} %weight.1, f32[4,4,256]{2,1,0:T(4,128)} %bitcast.5), custom_call_target="tpu_custom_call" | custom-call | tf_op jit(solution)/shard_map/mixing/pallas_call | solution.py:380

commit v6 on v5

--- a/solution.py
+++ b/solution.py
@@ -149,7 +149,7 @@
             snd[h, :, :, pl.ds(start, 16), :] = value.astype(BF16).reshape(n, jn, 16, LANES)
             return carry
 
-        lax.fori_loop(0, KMAX // 16, second, 0)
+        lax.fori_loop(0, KMAX // 16, second, 0, unroll=2)
 
     def exchange(src, dst, ssem, rsem, h):
         copies = []
@@ -179,7 +179,7 @@
                 mxo[h, q, j, pl.ds(start, 16), :] = parts[q].astype(BF16)
             return carry
 
-        lax.fori_loop(0, jn * (KMAX // 16), step, 0)
+        lax.fori_loop(0, jn * (KMAX // 16), step, 0, unroll=2)
         bck[h, me] = mxo[h, me]
 
     def inverse_mid(h):
@@ -194,7 +194,7 @@
                 z[:, pl.ds(start + i * 8, 8), :] = part.reshape(A, 8, LANES)
             return carry
 
-        lax.fori_loop(0, KMAX // 16, step, 0)
+        lax.fori_loop(0, KMAX // 16, step, 0, unroll=2)
 
     def inverse_rows(h, to, skip):
         def step(i, carry):

time: 120 us -> 118 us (0.983)
    pallas_call x1, Pallas kernels: 114 us -> 112 us  [local(): pl.pallas_call(functools.partial(filter_kernel, n, nc, halves, early), ou...]
where the time goes in v6:
time: 118 us
  Pallas kernels  118 us (100%)
    pallas_call x1, Pallas kernels, local(): pl.pallas_call(functools.partial(filter_kernel, n, nc, halves, early), ou...  112 us
    pallas_call x1, Pallas kernels, local(): pl.pallas_call(functools.partial(mixing_kernel, nc, halves, nb), out_shap...  5.69 us

profile of v6, /device:TPU:9, one launch (start us, length us, event | category | flops | bytes accessed | tf_op | source)
XLA Modules:
  0.0 117.8 jit_solution(13585715793299808684)
XLA Ops:
  0.0 112.1 %filter.1.gathered = bf16[2,4,8,256,128]{4,3,2,1,0:T(8,128)(2,1)} custom-call(bf16[32,256,256]{2,1,0:T(8,128)(2,1)} %bitcast.3, bf16[32,256,256]{2,1,0:T(8,128)(2,1)} %bitcast.4, f32[32,128,256]{2,1,0:T(8,128)} %gain.1, f32[8,256]{1,0:T(8,128)} %dgain.1, s32[16]{0:T(128)} %kept.1, bf16[256,256]{1,0:T(8,128)(2,1)} %constant.8.clone.band_hbm, ...), custom_call_target="tpu_custom_call" | custom-call | tf_op jit(solution)/shard_map/filter/pallas_call | solution.py:344
  112.1 5.7 %mixing.1 = bf16[2048,1024]{1,0:T(8,128)(2,1)} custom-call(bf16[2,4,8,256,128]{4,3,2,1,0:T(8,128)(2,1)} %filter.1.gathered, bf16[4,256,256]{2,1,0:T(8,128)(2,1)} %weight.1, f32[4,4,256]{2,1,0:T(4,128)} %bitcast.5), custom_call_target="tpu_custom_call" | custom-call | tf_op jit(solution)/shard_map/mixing/pallas_call | solution.py:380
